TPU v7x, 512 devices: a whole 4x8x8 slice. The times are simulated.
512 devices in a mesh: blk: 64 (over z_hi, y, core), group: 8 (over x, z_lo).
Axes of the slice: x: 4, y: 8, z: 8 (z_hi: 4, z_lo: 2; z = z_hi * 2 + z_lo), core: 2. Of those that a mesh axis runs over, the one named last changes fastest.
Arguments:
- activations: bfloat16 [65536, 2560], P(('blk', 'group')), may hold values from -6 to 6
- grad_out: bfloat16 [65536, 8192], P(('blk', 'group')), may hold values from -0.125 to 0.125
- kept_rows: int32 [512, 128], P(('blk', 'group')), may hold values from 0 to 19, as said below
- kept_cols: int32 [512, 128], P(('blk', 'group')), may hold values from 0 to 63, as said below
- kept_count: int32 [512], P(('blk', 'group')), may hold values from 2 to 128
- owner_tiles: int32 [1280], replicated, may hold values from 0 to 1279, as said below
- apply_mask: int32 [1280], P('blk'), may hold values 0 or 1
- feedback_in: bfloat16 [1280, 128, 128], P('blk'), may hold values from -4 to 4
Outputs:
- update: bfloat16 [1280, 128, 128], P('blk')
- feedback: bfloat16 [1280, 128, 128], P('blk')
Inputs may be any that keep to these rules, and one draw needn't show every extreme that they name: `kept_rows`: live entries of a worker name distinct tiles; of them at most 2 lie among the 20 tiles of any one owner (blk index p owns the tiles owner_tiles[p * 20] to owner_tiles[p * 20 + 19]). In every draw some worker has 2 tiles of every owner, and some owner has 2 tiles from every worker. Entries at kept_count and beyond are 0. `kept_cols`: as kept_rows, entry by entry. `owner_tiles`: A permutation of the tile numbers.
All inputs are finite; a program needn't handle non-finite values. No bound on the sum of `apply_mask` on one device may be relied on, other than what follows from the above.
Results may differ from a plain program's by a relative error of at most 0.0048.
Values may be sent and summed in bfloat16 or wider, within the bound.
A program may use at most 128 MiB of HBM per device.

v0:
```python
import jax
import jax.numpy as jnp
from jax import lax
from jax.sharding import PartitionSpec as P

SLOT = 2


def settle(summed, apply_mask):
    applied = (apply_mask == 1)[:, None, None]
    update = jnp.where(applied, summed, 0.0).astype(jnp.bfloat16)
    feedback = jnp.where(applied, 0.0, summed).astype(jnp.bfloat16)
    return (update, feedback)


def owner_sums(made_tiles, slot_labels, blocks, owned_tiles, tile_size):
    slot_count = blocks * SLOT
    received, got_labels = (
        lax.all_to_all(
            made_tiles.reshape(blocks, SLOT, tile_size, tile_size),
            "blk",
            split_axis=0,
            concat_axis=0,
            tiled=True,
        ),
        lax.all_to_all(
            slot_labels.reshape(blocks, SLOT), "blk", split_axis=0, concat_axis=0, tiled=True
        ),
    )
    label_ints = got_labels.reshape(slot_count).astype(jnp.int32)
    sorter = (label_ints[None, :] == jnp.arange(owned_tiles)[:, None]).astype(jnp.bfloat16)
    return jnp.dot(
        sorter,
        received.reshape(slot_count, tile_size * tile_size),
        preferred_element_type=jnp.float32,
    ).reshape(owned_tiles, tile_size, tile_size)


def on_device(
    activations, grad_out, kept_rows, kept_cols, kept_count, owner_tiles, apply_mask, feedback_in
):
    blocks = lax.axis_size("blk")
    owned_tiles = feedback_in.shape[0]
    tile_size = feedback_in.shape[1]
    tokens = activations.shape[0]
    tile_rows = activations.shape[1] // tile_size
    tile_cols = grad_out.shape[1] // tile_size
    everything = owner_tiles.shape[0]
    capacity = kept_rows.shape[1]
    slot_count = blocks * SLOT
    act_tiles = activations.reshape(tokens, tile_rows, tile_size)
    grad_tiles = grad_out.reshape(tokens, tile_cols, tile_size)
    row_list = kept_rows[0]
    col_list = kept_cols[0]
    places = (
        jnp.zeros((everything,), jnp.int32)
        .at[owner_tiles]
        .set(jnp.arange(everything, dtype=jnp.int32))
    )
    position = places[row_list * tile_cols + col_list]
    owner_pos = position // owned_tiles
    local_index = position % owned_tiles
    live_entry = jnp.arange(capacity) < kept_count[0]
    matches = ((owner_pos[:, None] == jnp.arange(blocks)[None, :]) & live_entry[:, None]).astype(
        jnp.int32
    )
    before = jnp.cumsum(matches, axis=0) - matches
    target = jnp.where(live_entry, owner_pos * SLOT + jnp.sum(before * matches, axis=1), -1)
    select = (target[None, :] == jnp.arange(slot_count)[:, None]).astype(jnp.int32)
    slot_row = jnp.sum(select * row_list[None, :], axis=1)
    slot_col = jnp.sum(select * col_list[None, :], axis=1)
    slot_live = jnp.sum(select, axis=1) > 0
    slot_labels = jnp.where(slot_live, jnp.sum(select * local_index[None, :], axis=1), -1).astype(
        jnp.bfloat16
    )
    picked_rows = jnp.take(act_tiles, slot_row, axis=1)
    picked_cols = jnp.take(grad_tiles, slot_col, axis=1)
    made_tiles = jnp.einsum(
        "ksa,ksb->sab", picked_rows, picked_cols, preferred_element_type=jnp.float32
    ).astype(jnp.bfloat16)
    owner_sum = owner_sums(made_tiles, slot_labels, blocks, owned_tiles, tile_size)
    group_total = lax.psum(owner_sum, "group")
    update, feedback = settle(group_total + feedback_in.astype(jnp.float32), apply_mask)
    return (update, feedback)


def solution(mesh):
    return jax.shard_map(
        on_device,
        mesh=mesh,
        in_specs=(
            P(("blk", "group"), None),
            P(("blk", "group"), None),
            P(("blk", "group"), None),
            P(("blk", "group"), None),
            P(("blk", "group")),
            P(),
            P("blk"),
            P("blk", None, None),
        ),
        out_specs=(P("blk", None, None), P("blk", None, None)),
        check_vma=False,
    )
```

profile of v0, /device:TPU:1, one launch (start us, length us, event | category | flops | bytes accessed | tf_op | source)
XLA Modules:
  0.0 321.7 jit_solution(6292667265251842628)
XLA Ops:
  7.2 0.0 copy-start
  8.0 0.7 fusion.22
  8.7 0.7 compare_select_fusion
  9.4 5.2 %scatter_custom_fusion = s32[1280]{0:T(1024)S(1)} fusion(s32[1280]{0:T(1024)S(1)} %compare_select_fusion, s32[1280]{0:T(1024)S(1)} %iota.23, s32[]{:T(128)} %constant.58.clone.1), kind=kCustom, calls=%fused_computation.35 | custom fusion | bytes 5124 | tf_op jit(solution)/shard_map/scatter | solution.py:58
  14.6 1.1 gather_fusion
  15.8 0.1 fusion.14
  15.9 0.2 reduce_window_sum.11
  16.1 0.2 select_reduce_fusion.3
  16.3 0.8 convert_reduce_fusion
  17.1 0.8 convert_element_type.54
  17.9 17.6 %all-to-all-start = ((bf16[64,1,2]{2,1,0:T(2,128)(2,1)}), bf16[64,1,2]{2,1,0:T(2,128)(2,1)S(1)}, u32[]{:S(2)}, u32[]{:S(2)}) async-start(bf16[64,1,2]{2,1,0:T(2,128)(2,1)} %convert_element_type.54), calls=%async_computation | async-start | bytes 65536 | tf_op jit(solution)/shard_map/all_to_all | solution.py:26
  35.6 1.4 copy.42
  37.0 0.3 copy.43
  37.3 0.0 copy-done
  37.4 2.5 copy.44
  39.8 3.2 copy.45
  43.0 3.1 gather_fusion.2
  46.1 3.1 gather_fusion.1
  49.2 7.2 %fusion.7 = bf16[128,128,128]{2,1,0:T(8,128)(2,1)} fusion(bf16[128,128,128]{2,1,0:T(8,128)(2,1)} %gather_fusion.2, pred[128]{0:T(512)(128)(4,1)S(1)} %get-tuple-element.20, bf16[128,128,128]{2,1,0:T(8,128)(2,1)} %gather_fusion.1, pred[128]{0:T(512)(128)(4,1)S(1)} %get-tuple-element.21), kind=kOutput, calls=%fused_computation.12 | convolution fusion | flops 543162368 | bytes 12583168 | tf_op jit(solution)/shard_map/ksa,ksb->sab/dot_general | solution.py:78
  56.4 0.0 all-to-all-done
  56.4 12.9 %all-to-all-start.1 = ((bf16[64,2,128,128]{3,2,1,0:T(8,128)(2,1)}), bf16[64,2,128,128]{3,2,1,0:T(8,128)(2,1)}, u32[]{:S(2)}, u32[]{:S(2)}) async-start(bf16[64,2,128,128]{3,2,1,0:T(8,128)(2,1)} %bitcast.46), calls=%async_computation.1 | async-start | bytes 8388608 | tf_op jit(solution)/shard_map/all_to_all | solution.py:19
  69.3 0.2 all-reduce.2.cloned.1.call-start
  69.5 0.1 convert_reduce_fusion.1
  69.7 0.1 reshape.172
  69.8 108.2 %all-to-all-done.1 = bf16[64,2,128,128]{3,2,1,0:T(8,128)(2,1)} async-done(((bf16[64,2,128,128]{3,2,1,0:T(8,128)(2,1)}), bf16[64,2,128,128]{3,2,1,0:T(8,128)(2,1)}, u32[]{:S(2)}, u32[]{:S(2)}) %all-to-all-start.1) | async-done | bytes 4194336 | tf_op jit(solution)/shard_map/all_to_all | solution.py:19
  177.9 7.7 %copy.56 = bf16[16,8,128,128]{3,1,2,0:T(8,128)(2,1)} copy(bf16[16,8,128,128]{3,2,1,0:T(8,128)(2,1)} %bitcast.19) | data formatting | bytes 8388608
  185.6 6.4 %copy.47 = bf16[128,16384]{0,1:T(8,128)(2,1)} copy(bf16[128,16384]{1,0:T(8,128)(2,1)} %bitcast.44) | data formatting | bytes 8388608 | tf_op jit(solution)/shard_map/reshape | solution.py:34
  192.0 0.0 copy-start.2
  192.0 0.0 copy-start.1
  192.0 4.6 %fusion.16 = f32[20,128,128]{2,0,1:T(8,128)} fusion(bf16[128,128,128]{2,1,0:T(8,128)(2,1)} %bitcast.43, s32[128]{0:T(128)S(1)} %reshape.172), kind=kOutput, calls=%fused_computation.30 | convolution fusion | flops 83888640 | bytes 5505536 | tf_op jit(solution)/shard_map/dot_general | solution.py:32
  196.6 0.0 all-reduce.2.cloned.1.call-update
  196.6 0.0 copy-done.2
  196.6 114.3 %all-reduce.2.cloned.1.call-done = f32[20,128,128]{2,0,1:T(8,128)} async-done(((f32[20,128,128]{2,0,1:T(8,128)}), f32[20,128,128]{2,0,1:T(8,128)}) %all-reduce.2.cloned.1.call-update) | async-done | bytes 1310736 | tf_op jit(solution)/shard_map/psum | solution.py:82
  310.9 0.0 copy-done.1
  310.9 2.0 select_convert_fusion
  312.9 1.0 copy.50
  313.9 1.0 copy.49
  (11 shorter events, 0.1 us)
Async XLA Ops:
  7.2 30.2 %copy-start = (bf16[128,8192]{1,0:T(8,128)(2,1)S(1)}, bf16[128,8192]{1,0:T(8,128)(2,1)}, u32[]{:S(2)}) copy-start(bf16[128,8192]{1,0:T(8,128)(2,1)} %param.9) | copy-start | bytes 6291460
  17.9 38.5 %all-to-all-start = ((bf16[64,1,2]{2,1,0:T(2,128)(2,1)}), bf16[64,1,2]{2,1,0:T(2,128)(2,1)S(1)}, u32[]{:S(2)}, u32[]{:S(2)}) async-start(bf16[64,1,2]{2,1,0:T(2,128)(2,1)} %convert_element_type.54), calls=%async_computation | async-start | bytes 65536 | tf_op jit(solution)/shard_map/all_to_all | solution.py:26
  56.4 121.6 %all-to-all-start.1 = ((bf16[64,2,128,128]{3,2,1,0:T(8,128)(2,1)}), bf16[64,2,128,128]{3,2,1,0:T(8,128)(2,1)}, u32[]{:S(2)}, u32[]{:S(2)}) async-start(bf16[64,2,128,128]{3,2,1,0:T(8,128)(2,1)} %bitcast.46), calls=%async_computation.1 | async-start | bytes 8388608 | tf_op jit(solution)/shard_map/all_to_all | solution.py:19
  69.3 241.6 %all-reduce.2.cloned.1.call-start = ((), (), s32[]{:S(2)}) async-start(), calls=%async_computation.2 | async-start | bytes 3145728 | tf_op jit(solution)/shard_map/psum | solution.py:82
  192.0 4.6 %copy-start.2 = (s32[20]{0:T(128)S(1)}, s32[20]{0:T(128)}, u32[]{:S(2)}) copy-start(s32[20]{0:T(128)} %param.14) | copy-start | bytes 244
  192.0 118.9 %copy-start.1 = (bf16[20,128,128]{2,1,0:T(8,128)(2,1)S(1)}, bf16[20,128,128]{2,1,0:T(8,128)(2,1)}, u32[]{:S(2)}) copy-start(bf16[20,128,128]{2,1,0:T(8,128)(2,1)} %param.15) | copy-start | bytes 1966084
Sparse Core Ops, SparseCore 0:
  196.7 114.1 all-reduce.1
where the time goes:
time: 324 us; the launch traced here: 322 us
  waiting for transfers between devices  222 us (69%)
  local copies, waits for them, and re-layouts  36.9 us (11%)
  starting transfers between devices  30.8 us (10%)
  between operations  15 us (5%)
  matrix products  11.8 us (4%)
  other arithmetic  4.82 us (1%)
    psum x1, waiting for transfers between devices, on_device(): group_total = lax.psum(owner_sum, 'group')  114 us
    all_to_all x1, waiting for transfers between devices, owner_sums(): lax.all_to_all(made_tiles.reshape(blocks, SLOT, tile_size, tile_size), 'b...  108 us
    all_to_all x1, starting transfers between devices, owner_sums(): lax.all_to_all(slot_labels.reshape(blocks, SLOT), 'blk', split_axis=0, co...  17.6 us
    unnamed x11, local copies, waits for them, and re-layouts  13.5 us
    all_to_all x1, starting transfers between devices, owner_sums(): lax.all_to_all(made_tiles.reshape(blocks, SLOT, tile_size, tile_size), 'b...  12.9 us
    dot_general x1, matrix products, on_device(): jnp.einsum('ksa,ksb->sab', picked_rows, picked_cols, preferred_element_ty...  7.22 us
  transfers between devices with their start and end apart: 3, of which 2 were waited for; matrix products, arithmetic and copies ran while one was open for 7% of the time, Pallas kernels for 0%

commit v1 on v0

v1 whole, which is shorter than its diff:
```python
import functools

import jax
import jax.numpy as jnp
from jax import lax
from jax.experimental import pallas as pl
from jax.experimental.pallas import tpu as pltpu
from jax.sharding import PartitionSpec as P

ZH, YN, CORES, XN, ZL = 4, 8, 2, 4, 2
SLICES = XN * ZL
CLUSTER = SLICES * CORES
SLOT = 2
TILE = 128
ROWS = TILE // SLICES
OWNED = 20
PIECE = OWNED * ROWS
PER_CHUNK = YN * SLOT
MESH = pl.DeviceIdType.MESH
F32 = jnp.float32
BF16 = jnp.bfloat16


def prep_kernel(count_ref, rows_ref, cols_ref, tiles_ref, table_ref, code_ref):
    n = TILE
    sub = lax.broadcasted_iota(jnp.int32, (n, n), 0).astype(F32)
    lane = lax.broadcasted_iota(jnp.int32, (n, n), 1).astype(F32)
    count = count_ref[0].astype(F32)
    row_of = jnp.broadcast_to(rows_ref[...].astype(F32), (n, n)).T
    col_of = jnp.broadcast_to(cols_ref[...].astype(F32), (n, n)).T
    tile_of = row_of * 64.0 + col_of
    found = jnp.zeros((n, n), F32)
    for k in range(tiles_ref.shape[0]):
        known = tiles_ref[k : k + 1, :].astype(F32)
        found += jnp.where(tile_of == known, lane + 128.0 * k, 0.0)
    position = jnp.broadcast_to(jnp.sum(found, axis=1, keepdims=True), (n, n))
    owner = jnp.floor((position + 0.5) * (1.0 / OWNED))
    label = position - OWNED * owner
    same = (owner.T == owner) & (lane < sub) & (lane < count)
    rank = jnp.sum(jnp.where(same, 1.0, 0.0), axis=1, keepdims=True)
    z_hi = jnp.floor((owner + 0.5) * (1.0 / 16.0))
    in_plane = owner - 16.0 * z_hi
    y = jnp.floor((in_plane + 0.5) * 0.5)
    core = in_plane - 2.0 * y
    slot = ((z_hi * 2.0 + core) * 8.0 + y) * 2.0 + rank
    chosen = (slot == lane) & (sub < count)
    slot_row = jnp.sum(jnp.where(chosen, row_of, 0.0), axis=0, keepdims=True)
    slot_col = jnp.sum(jnp.where(chosen, col_of, 0.0), axis=0, keepdims=True)
    slot_label = jnp.sum(jnp.where(chosen, label + 1.0, 0.0), axis=0, keepdims=True) - 1.0
    table_ref[0:1, :] = slot_row.astype(jnp.int32)
    table_ref[1:2, :] = slot_col.astype(jnp.int32)
    m = CORES * ZH * YN
    at = lax.broadcasted_iota(jnp.int32, (m, n), 0)
    s = lax.broadcasted_iota(jnp.int32, (m, n), 1)
    want = ((at // 8) % 4 * 2 + at // 32) * 8 + at % 8
    spread = jnp.where(s // 2 == want, jnp.broadcast_to(slot_label, (m, n)), 0.0).astype(BF16)
    s2 = lax.broadcasted_iota(jnp.int32, (n, n), 0)
    l2 = lax.broadcasted_iota(jnp.int32, (n, n), 1)
    pick = jnp.where(s2 % 2 == (l2 % 32) // 16, 1.0, 0.0).astype(BF16)
    coded = jnp.dot(spread, pick, preferred_element_type=F32) * 16.0
    coded += (lax.broadcasted_iota(jnp.int32, (m, n), 1) % 16).astype(F32)
    code_ref[...] = coded.reshape(CORES, ZH, YN, n)


def main_kernel(
    table_ref, code_ref, act_ref, grad_ref, back_ref, out_ref,
    act_t, grad_t, made, got, codes, keys, sums, to_right, from_left, to_left, from_right, to_z, from_z,
    code_send, code_recv, made_send, made_recv,
    right_send, right_recv, left_send, left_recv, z_send, z_recv, out_send, out_recv,
):
    blk = lax.axis_index("blk")
    group = lax.axis_index("group")
    z_hi, y, core = blk // 16, (blk // 2) % 8, blk % 2
    x, z_lo = group // 2, group % 2
    me = group * 2 + core

    def device(z_hi_at, y_at, core_at, group_at):
        return ((z_hi_at * 8 + y_at) * 2 + core_at, group_at)

    def peer(n, way):
        dx, dz, dc = n // 4, (n // 2) % 2, n % 2
        return ((x + way * dx + XN) % XN) * 2 + (z_lo + dz) % 2, (core + dc) % 2

    right = device(z_hi, (y + 1) % 8, core, group)
    left = device(z_hi, (y + 7) % 8, core, group)

    barrier = pltpu.get_barrier_semaphore()

    def greet(n, _):
        g, c = peer(n, 1)
        pl.semaphore_signal(barrier, inc=1, device_id=device(z_hi, y, c, g), device_id_type=MESH)
        return 0

    lax.fori_loop(1, CLUSTER, greet, 0)
    for there in (right, left):
        pl.semaphore_signal(barrier, inc=1, device_id=there, device_id_type=MESH)
    for k in range(1, ZH):
        pl.semaphore_signal(
            barrier, inc=1, device_id=device((z_hi + k) % 4, y, core, group), device_id_type=MESH
        )

    def turn(r, _):
        at = pl.ds(pl.multiple_of(r * TILE, TILE), TILE)
        act_t[r] = act_ref[:, at].T
        return 0

    lax.fori_loop(0, act_ref.shape[1] // TILE, turn, 0)

    def part(r, _):
        grad_t[r] = grad_ref[:, pl.ds(pl.multiple_of(r * TILE, TILE), TILE)]
        return 0

    lax.fori_loop(0, grad_ref.shape[1] // TILE, part, 0)

    def make(k):
        z_to = (z_hi + 1 + k) % 4

        def one(s, _):
            c, slot = s // PER_CHUNK, s % PER_CHUNK
            e = z_to * (CORES * PER_CHUNK) + s
            a, b = act_t[table_ref[0, e]], grad_t[table_ref[1, e]]
            tile = jnp.dot(a, b, preferred_element_type=F32).astype(BF16)
            made[k, c, :, slot] = tile.reshape(SLICES, ROWS, TILE)
            return 0

        lax.fori_loop(0, CORES * PER_CHUNK, one, 0, unroll=4)

    def code_copy(n, way):
        g, c = peer(n, way)
        return pltpu.make_async_remote_copy(
            src_ref=code_ref.at[c],
            dst_ref=codes.at[me if way == 1 else g * 2 + c],
            send_sem=code_send.at[n],
            recv_sem=code_recv.at[n],
            device_id=device(z_hi, y, c, g),
            device_id_type=MESH,
        )

    def made_copy(k, n, way):
        g, c = peer(n, way)
        return pltpu.make_async_remote_copy(
            src_ref=made.at[k, c, g],
            dst_ref=got.at[k, me if way == 1 else g * 2 + c],
            send_sem=made_send.at[k, n],
            recv_sem=made_recv.at[k, n],
            device_id=device(z_hi, y, c, g),
            device_id_type=MESH,
        )

    def each_peer(do):
        def step(n, _):
            do(n)
            return 0

        lax.fori_loop(1, CLUSTER, step, 0)

    make(0)
    pl.semaphore_wait(barrier, CLUSTER - 1 + 2 + ZH - 1)
    each_peer(lambda n: code_copy(n, 1).start())
    each_peer(lambda n: made_copy(0, n, 1).start())
    codes[me] = code_ref[core]
    for k in range(1, ZH):
        make(k)
        each_peer(lambda n, k=k: made_copy(k, n, 1).start())
    for k in range(ZH):
        got[k, me] = made[k, core, group]
    each_peer(lambda n: code_copy(n, -1).wait_recv())

    lane = lax.broadcasted_iota(jnp.int32, (YN, TILE), 1)
    row = lax.broadcasted_iota(jnp.int32, (PIECE, CLUSTER * SLOT * ROWS), 0).astype(F32)

    def right_copy(k, s):
        return pltpu.make_async_remote_copy(
            src_ref=to_right.at[k, s], dst_ref=from_left.at[k, s],
            send_sem=right_send.at[k, s], recv_sem=right_recv.at[k, s],
            device_id=right, device_id_type=MESH,
        )

    def left_copy(k, s):
        return pltpu.make_async_remote_copy(
            src_ref=to_left.at[k, s], dst_ref=from_right.at[k, s],
            send_sem=left_send.at[k, s], recv_sem=left_recv.at[k, s],
            device_id=left, device_id_type=MESH,
        )

    def z_copy(k):
        return pltpu.make_async_remote_copy(
            src_ref=to_z.at[k], dst_ref=from_z.at[k],
            send_sem=z_send.at[k], recv_sem=z_recv.at[k],
            device_id=device((z_hi + 1 + k) % 4, y, core, group), device_id_type=MESH,
        )

    total = None
    for k in range(ZH):
        z_to = (z_hi + 1 + k) % 4
        each_peer(lambda n, k=k: made_copy(k, n, -1).wait_recv())
        for kk in range(4):
            key = jnp.zeros((YN, TILE), F32)
            for i in range(4):
                key = jnp.where(lane // 32 == i, codes[kk * 4 + i, z_to], key)
            keys[:, kk * TILE : (kk + 1) * TILE] = key

        def sum_owner(d, _, k=k):
            key = keys[pl.ds(d, 1), :]
            pick = jnp.where(row == key, 1.0, 0.0).astype(BF16)
            parts = got[k, :, pl.ds(d * SLOT, SLOT)].reshape(CLUSTER * SLOT * ROWS, TILE)
            sums[k, d] = jnp.dot(pick, parts, preferred_element_type=F32)
            return 0

        lax.fori_loop(0, YN, sum_owner, 0)

        for s in range(4):
            part = sums[k, (y + 4 - s) % 8]
            if s > 0:
                right_copy(k, s - 1).wait_recv()
                part += from_left[k, s - 1].astype(F32)
            to_right[k, s] = part.astype(BF16)
            right_copy(k, s).start()
            if s < 3:
                part = sums[k, (y + 5 + s) % 8]
                if s > 0:
                    left_copy(k, s - 1).wait_recv()
                    part += from_right[k, s - 1].astype(F32)
                to_left[k, s] = part.astype(BF16)
                left_copy(k, s).start()
        total = sums[k, y]
        left_copy(k, 2).wait_recv()
        total += from_right[k, 2].astype(F32)
        right_copy(k, 3).wait_recv()
        total += from_left[k, 3].astype(F32)
        if k < ZH - 1:
            to_z[k] = total.astype(BF16)
            z_copy(k).start()

    for k in range(ZH - 1):
        z_copy(k).wait_recv()
        total += from_z[k].astype(F32)
    mine = pl.ds(pl.multiple_of(group * ROWS, ROWS), ROWS)
    total += back_ref[:, mine, :].astype(F32).reshape(PIECE, TILE)
    out_ref[:, mine, :] = total.astype(BF16).reshape(OWNED, ROWS, TILE)

    def out_copy(n, way):
        g = (group + way * n + SLICES) % SLICES
        at = group if way == 1 else g
        there = out_ref.at[:, pl.ds(pl.multiple_of(at * ROWS, ROWS), ROWS), :]
        return pltpu.make_async_remote_copy(
            src_ref=there, dst_ref=there,
            send_sem=out_send.at[n], recv_sem=out_recv.at[n],
            device_id=device(z_hi, y, core, g), device_id_type=MESH,
        )

    def each_slice(do):
        def step(n, _):
            do(n)
            return 0

        lax.fori_loop(1, SLICES, step, 0)

    each_slice(lambda n: out_copy(n, 1).start())
    each_slice(lambda n: out_copy(n, -1).wait_recv())

    each_peer(lambda n: code_copy(n, 1).wait_send())
    for k in range(ZH):
        each_peer(lambda n, k=k: made_copy(k, n, 1).wait_send())
        for s in range(4):
            right_copy(k, s).wait_send()
        for s in range(3):
            left_copy(k, s).wait_send()
        if k < ZH - 1:
            z_copy(k).wait_send()
    each_slice(lambda n: out_copy(n, 1).wait_send())


def on_device(
    activations, grad_out, kept_rows, kept_cols, kept_count, owner_tiles, apply_mask, feedback_in
):
    vmem = pl.BlockSpec(memory_space=pltpu.VMEM)
    smem = pl.BlockSpec(memory_space=pltpu.SMEM)
    table, code = pl.pallas_call(
        prep_kernel,
        out_shape=(
            jax.ShapeDtypeStruct((2, TILE), jnp.int32),
            jax.ShapeDtypeStruct((CORES, ZH, YN, TILE), F32),
        ),
        in_specs=[smem, vmem, vmem, vmem],
        out_specs=(vmem, vmem),
    )(kept_count, kept_rows, kept_cols, owner_tiles.reshape(-1, TILE))

    dma = pltpu.SemaphoreType.DMA
    summed = pl.pallas_call(
        main_kernel,
        out_shape=jax.ShapeDtypeStruct(feedback_in.shape, BF16),
        in_specs=[smem, vmem, vmem, vmem, vmem],
        out_specs=vmem,
        scratch_shapes=[
            pltpu.VMEM((activations.shape[1] // TILE, TILE, TILE), BF16),
            pltpu.VMEM((grad_out.shape[1] // TILE, TILE, TILE), BF16),
            pltpu.VMEM((ZH, CORES, SLICES, PER_CHUNK, ROWS, TILE), BF16),
            pltpu.VMEM((ZH, CLUSTER, PER_CHUNK, ROWS, TILE), BF16),
            pltpu.VMEM((CLUSTER, ZH, YN, TILE), F32),
            pltpu.VMEM((YN, CLUSTER * SLOT * ROWS), F32),
            pltpu.VMEM((ZH, YN, PIECE, TILE), F32),
            pltpu.VMEM((ZH, 4, PIECE, TILE), BF16),
            pltpu.VMEM((ZH, 4, PIECE, TILE), BF16),
            pltpu.VMEM((ZH, 3, PIECE, TILE), BF16),
            pltpu.VMEM((ZH, 3, PIECE, TILE), BF16),
            pltpu.VMEM((ZH - 1, PIECE, TILE), BF16),
            pltpu.VMEM((ZH - 1, PIECE, TILE), BF16),
            dma((CLUSTER,)), dma((CLUSTER,)),
            dma((ZH, CLUSTER)), dma((ZH, CLUSTER)),
            dma((ZH, 4)), dma((ZH, 4)),
            dma((ZH, 3)), dma((ZH, 3)),
            dma((ZH - 1,)), dma((ZH - 1,)),
            dma((SLICES,)), dma((SLICES,)),
        ],
        compiler_params=pltpu.CompilerParams(
            collective_id=0, has_side_effects=True, vmem_limit_bytes=56 * 2**20
        ),
    )(table, code, activations, grad_out, feedback_in)
    applied = (apply_mask == 1)[:, None, None]
    zero = jnp.zeros((), BF16)
    return (jnp.where(applied, summed, zero), jnp.where(applied, zero, summed))


def solution(mesh):
    return jax.shard_map(
        on_device,
        mesh=mesh,
        in_specs=(
            P(("blk", "group"), None),
            P(("blk", "group"), None),
            P(("blk", "group"), None),
            P(("blk", "group"), None),
            P(("blk", "group")),
            P(),
            P("blk"),
            P("blk", None, None),
        ),
        out_specs=(P("blk", None, None), P("blk", None, None)),
        check_vma=False,
    )
```

time: 324 us -> 117 us (0.36)
  the two profiles are of different devices: /device:TPU:1 before, /device:TPU:32 now
where the time goes in v1:
time: 117 us
  Pallas kernels  113 us (97%)
  other arithmetic  2.96 us (3%)
  between operations  1.29 us (1%)
    pallas_call x1, Pallas kernels, on_device(): pl.pallas_call(main_kernel, out_shape=jax.ShapeDtypeStruct(feedback_in.sh...  111 us

profile of v1, /device:TPU:32, one launch (start us, length us, event | category | flops | bytes accessed | tf_op | source)
XLA Modules:
  0.0 116.9 jit_solution(2237354030686549187)
XLA Ops:
  1.3 0.7 broadcast_compare_fusion
  1.9 1.9 %shard_map.95 = (s32[2,128]{1,0:T(2,128)}, f32[2,4,8,128]{3,2,1,0:T(8,128)}) custom-call(s32[1]{0:T(128)S(6)} %copy.10.count_ref, s32[1,128]{1,0:T(1,128)} %rows_ref.1, s32[1,128]{1,0:T(1,128)} %cols_ref.1, s32[10,128]{1,0:T(8,128)} %bitcast.1), custom_call_target="tpu_custom_call" | custom-call | tf_op jit(solution)/shard_map/pallas_call | solution.py:279
  3.8 110.8 %shard_map.96 = bf16[20,128,128]{2,1,0:T(8,128)(2,1)} custom-call(s32[2,128]{1,0:T(2,128)} %get-tuple-element.4.table_ref, f32[2,4,8,128]{3,2,1,0:T(8,128)} %get-tuple-element.5.code_ref, bf16[128,2560]{1,0:T(8,128)(2,1)} %act_ref.1, bf16[128,8192]{1,0:T(8,128)(2,1)} %grad_ref.1, bf16[20,128,128]{2,1,0:T(8,128)(2,1)} %back_ref.1), custom_call_target="tpu_custom_call" | custom-call | tf_op jit(solution)/shard_map/pallas_call | solution.py:290
  114.6 2.3 %broadcast_select_fusion = (bf16[20,128,128]{2,1,0:T(8,128)(2,1)}, bf16[20,128,128]{2,1,0:T(8,128)(2,1)}) fusion(bf16[20,128,128]{2,1,0:T(8,128)(2,1)} %shard_map.96, pred[20]{0:T(512)(128)(4,1)S(1)} %broadcast_compare_fusion), kind=kLoop, calls=%fused_computation | loop fusion | flops 655360 | bytes 1966100 | tf_op jit(solution)/shard_map/jit(_where)/select_n | solution.py:322

commit v2 on v1

v2 whole, which is shorter than its diff:
```python
import functools

import jax
import jax.numpy as jnp
from jax import lax
from jax.experimental import pallas as pl
from jax.experimental.pallas import tpu as pltpu
from jax.sharding import PartitionSpec as P

ZH, YN, CORES, XN, ZL = 4, 8, 2, 4, 2
SLICES = XN * ZL
CLUSTER = SLICES * CORES
SLOT = 2
TILE = 128
ROWS = TILE // SLICES
OWNED = 20
PIECE = OWNED * ROWS
PER_CHUNK = YN * SLOT
PARTS = 16
AHEAD = 6
MESH = pl.DeviceIdType.MESH
F32 = jnp.float32
BF16 = jnp.bfloat16


def prep_kernel(count_ref, rows_ref, cols_ref, tiles_ref, table_ref, code_ref):
    n = TILE
    sub = lax.broadcasted_iota(jnp.int32, (n, n), 0).astype(F32)
    lane = lax.broadcasted_iota(jnp.int32, (n, n), 1).astype(F32)
    count = count_ref[0].astype(F32)
    row_of = jnp.broadcast_to(rows_ref[...].astype(F32), (n, n)).T
    col_of = jnp.broadcast_to(cols_ref[...].astype(F32), (n, n)).T
    tile_of = row_of * 64.0 + col_of
    found = jnp.zeros((n, n), F32)
    for k in range(tiles_ref.shape[0]):
        known = tiles_ref[k : k + 1, :].astype(F32)
        found += jnp.where(tile_of == known, lane + 128.0 * k, 0.0)
    position = jnp.broadcast_to(jnp.sum(found, axis=1, keepdims=True), (n, n))
    owner = jnp.floor((position + 0.5) * (1.0 / OWNED))
    label = position - OWNED * owner
    same = (owner.T == owner) & (lane < sub) & (lane < count)
    rank = jnp.sum(jnp.where(same, 1.0, 0.0), axis=1, keepdims=True)
    z_hi = jnp.floor((owner + 0.5) * (1.0 / 16.0))
    in_plane = owner - 16.0 * z_hi
    y = jnp.floor((in_plane + 0.5) * 0.5)
    core = in_plane - 2.0 * y
    slot = ((z_hi * 2.0 + core) * 8.0 + y) * 2.0 + rank
    chosen = (slot == lane) & (sub < count)
    slot_row = jnp.sum(jnp.where(chosen, row_of, 0.0), axis=0, keepdims=True)
    slot_col = jnp.sum(jnp.where(chosen, col_of, 0.0), axis=0, keepdims=True)
    slot_label = jnp.sum(jnp.where(chosen, label + 1.0, 0.0), axis=0, keepdims=True) - 1.0
    table_ref[0:1, :] = slot_row.astype(jnp.int32)
    table_ref[1:2, :] = slot_col.astype(jnp.int32)
    m = CORES * YN
    at = lax.broadcasted_iota(jnp.int32, (m, n), 0)
    s = lax.broadcasted_iota(jnp.int32, (m, n), 1)
    mine = (s // 16) % 2 * 8 + (s // 2) % 8 == at
    spread = jnp.where(mine, jnp.broadcast_to(slot_label, (m, n)), 0.0).astype(BF16)
    s2 = lax.broadcasted_iota(jnp.int32, (n, n), 0)
    l2 = lax.broadcasted_iota(jnp.int32, (n, n), 1)
    pick = jnp.where((s2 // 32 == l2 // 32) & (s2 % 2 == l2 // 16 % 2), 1.0, 0.0).astype(BF16)
    coded = jnp.dot(spread, pick, preferred_element_type=F32) * 16.0
    coded += (lax.broadcasted_iota(jnp.int32, (m, n), 1) % 16).astype(F32)
    code_ref[...] = coded.reshape(CORES, YN, n)


def main_kernel(
    table_ref, code_ref, act_ref, grad_ref, back_ref, out_ref,
    act_t, grad_t, other, made, got, codes, keys, own,
    to_right, from_left, to_left, from_right, to_z, from_z,
    code_send, code_recv, swap_send, swap_recv, made_send, made_recv,
    right_send, right_recv, left_send, left_recv, z_send, z_recv, out_send, out_recv,
):
    blk = lax.axis_index("blk")
    group = lax.axis_index("group")
    z_hi, y, core = blk // 16, (blk // 2) % 8, blk % 2
    x, z_lo = group // 2, group % 2
    me = group * 2 + core

    def device(z_hi_at, y_at, core_at, group_at):
        return ((z_hi_at * 8 + y_at) * 2 + core_at, group_at)

    def member(n, way):
        return ((x + way * (n // 2) + XN) % XN) * 2 + (z_lo + n % 2) % 2

    def remote(src, dst, send, recv, to):
        return pltpu.make_async_remote_copy(
            src_ref=src, dst_ref=dst, send_sem=send, recv_sem=recv,
            device_id=to, device_id_type=MESH,
        )

    def each(stop, do):
        def step(n, _):
            do(n)
            return 0

        lax.fori_loop(1, stop, step, 0)

    right = device(z_hi, (y + 1) % 8, core, group)
    left = device(z_hi, (y + 7) % 8, core, group)
    sibling = device(z_hi, y, 1 - core, group)

    barrier = pltpu.get_barrier_semaphore()

    def greet(to):
        pl.semaphore_signal(barrier, inc=1, device_id=to, device_id_type=MESH)

    each(CLUSTER, lambda n: greet(device(z_hi, y, (core + n % 2) % 2, member(n // 2, 1))))
    greet(right)
    greet(left)
    each(ZH, lambda k: greet(device((z_hi + k) % 4, y, core, group)))

    def turn(r, _):
        act_t[r] = act_ref[:, pl.ds(pl.multiple_of(r * TILE, TILE), TILE)].T
        return 0

    lax.fori_loop(0, act_ref.shape[1] // TILE, turn, 0, unroll=4)

    def part(r, _):
        grad_t[r] = grad_ref[:, pl.ds(pl.multiple_of(r * TILE, TILE), TILE)]
        return 0

    lax.fori_loop(0, grad_ref.shape[1] // TILE, part, 0, unroll=4)

    def order(m):
        return m // 8 * 2 + m % 2, m // 2 % 4

    def plane(k):
        return (z_hi + 1 + k) % 4

    def pair(p):
        return (y + 4 - p) % 8, (y + 5 + p) % 8

    def make(m):
        k, p = order(m)

        def tile(c, o, j):
            e = (plane(k) * 2 + c) * PER_CHUNK + pair(p)[o] * SLOT + j
            a, b = act_t[table_ref[0, e]], grad_t[table_ref[1, e]]
            product = jnp.dot(a, b, preferred_element_type=F32).astype(BF16)
            return product.reshape(SLICES, ROWS, TILE)

        for o in range(2):
            for j in range(SLOT):
                other[m, :, o * SLOT + j] = tile(1 - core, o, j)
        for o in range(2):
            for j in range(SLOT):
                made[m, :, core, o * SLOT + j] = tile(core, o, j)

    def code_copy(n, way):
        g, c = member(n // 2, way), (core + n % 2) % 2
        return remote(
            code_ref.at[c], codes.at[me if way == 1 else g * 2 + c],
            code_send.at[n], code_recv.at[n], device(z_hi, y, c, g),
        )

    def swap(m, way):
        there = made.at[m, :, core if way == 1 else 1 - core]
        return remote(other.at[m], there, swap_send.at[m], swap_recv.at[m], sibling)

    def made_copy(m, n, way):
        g = member(n, way)
        return remote(
            made.at[m, g], got.at[m, group if way == 1 else g],
            made_send.at[m, n], made_recv.at[m, n], device(z_hi, y, core, g),
        )

    def right_copy(k, s):
        return remote(
            to_right.at[k, s], from_left.at[k, s], right_send.at[k, s], right_recv.at[k, s], right
        )

    def left_copy(k, s):
        return remote(
            to_left.at[k, s], from_right.at[k, s], left_send.at[k, s], left_recv.at[k, s], left
        )

    def z_copy(k):
        to = device(plane(k), y, core, group)
        return remote(to_z.at[k], from_z.at[k], z_send.at[k], z_recv.at[k], to)

    def out_copy(n, way):
        g = member(n, way)
        at = group if way == 1 else g
        there = out_ref.at[:, pl.ds(pl.multiple_of(at * ROWS, ROWS), ROWS), :]
        return remote(there, there, out_send.at[n], out_recv.at[n], device(z_hi, y, core, g))

    def send(m):
        swap(m, -1).wait_recv()
        each(SLICES, lambda n: made_copy(m, n, 1).start())

    lane = lax.broadcasted_iota(jnp.int32, (YN, TILE), 1)
    row = lax.broadcasted_iota(jnp.int32, (PIECE, CLUSTER * SLOT * ROWS), 0).astype(F32)

    def line_up(k):
        for kk in range(4):
            key = jnp.zeros((YN, TILE), F32)
            for i in range(4):
                turned = pltpu.roll(codes[kk * 4 + i], (i + 4 - plane(k)) % 4 * 32, 1)
                key = jnp.where(lane // 32 == i, turned, key)
            keys[k, :, kk * TILE : (kk + 1) * TILE] = key

    def owner_sum(m, o):
        k, p = order(m)
        pick = jnp.where(row == keys[k, pl.ds(pair(p)[o], 1), :], 1.0, 0.0).astype(BF16)
        parts = got[m, :, :, o * SLOT : (o + 1) * SLOT].reshape(CLUSTER * SLOT * ROWS, TILE)
        return jnp.dot(pick, parts, preferred_element_type=F32)

    def finish(k):
        left_copy(k, 2).wait_recv()
        right_copy(k, 3).wait_recv()
        total = own[k] + from_right[k, 2].astype(F32) + from_left[k, 3].astype(F32)
        if k < ZH - 1:
            to_z[k] = total.astype(BF16)
            z_copy(k).start()
        return total

    make(0)
    pl.semaphore_wait(barrier, CLUSTER - 1 + 2 + ZH - 1)
    swap(0, 1).start()
    each(CLUSTER, lambda n: code_copy(n, 1).start())
    codes[me] = code_ref[core]
    for m in range(1, AHEAD + 1):
        make(m)
        swap(m, 1).start()
        send(m - 1)
    each(CLUSTER, lambda n: code_copy(n, -1).wait_recv())
    for k in range(ZH):
        line_up(k)

    total = None
    for m in range(PARTS):
        k, p = order(m)
        if m + AHEAD + 1 < PARTS:
            make(m + AHEAD + 1)
            swap(m + AHEAD + 1, 1).start()
        if m + AHEAD < PARTS:
            send(m + AHEAD)
        got[m, group] = made[m, group]
        each(SLICES, lambda n, m=m: made_copy(m, n, -1).wait_recv())
        rightward = owner_sum(m, 0)
        if p > 0:
            right_copy(k, p - 1).wait_recv()
            rightward += from_left[k, p - 1].astype(F32)
        to_right[k, p] = rightward.astype(BF16)
        right_copy(k, p).start()
        leftward = owner_sum(m, 1)
        if p < 3:
            if p > 0:
                left_copy(k, p - 1).wait_recv()
                leftward += from_right[k, p - 1].astype(F32)
            to_left[k, p] = leftward.astype(BF16)
            left_copy(k, p).start()
        else:
            own[k] = leftward
        if m > 0 and order(m - 1)[1] == 3:
            finish(order(m - 1)[0])
    total = finish(ZH - 1)

    for k in range(ZH - 1):
        z_copy(k).wait_recv()
        total += from_z[k].astype(F32)
    mine = pl.ds(pl.multiple_of(group * ROWS, ROWS), ROWS)
    total += back_ref[:, mine, :].astype(F32).reshape(PIECE, TILE)
    out_ref[:, mine, :] = total.astype(BF16).reshape(OWNED, ROWS, TILE)
    each(SLICES, lambda n: out_copy(n, 1).start())
    each(SLICES, lambda n: out_copy(n, -1).wait_recv())

    each(CLUSTER, lambda n: code_copy(n, 1).wait_send())
    for m in range(PARTS):
        swap(m, 1).wait_send()
        each(SLICES, lambda n, m=m: made_copy(m, n, 1).wait_send())
    for k in range(ZH):
        for s in range(4):
            right_copy(k, s).wait_send()
        for s in range(3):
            left_copy(k, s).wait_send()
        if k < ZH - 1:
            z_copy(k).wait_send()
    each(SLICES, lambda n: out_copy(n, 1).wait_send())


def split_kernel(mask_ref, summed_ref, update_ref, feedback_ref):
    rows = summed_ref.shape[0]
    for t in range(rows):
        applied = mask_ref[pl.program_id(0) * rows + t] == 1
        summed = summed_ref[t].astype(F32)
        update_ref[t] = jnp.where(applied, summed, 0.0).astype(BF16)
        feedback_ref[t] = jnp.where(applied, 0.0, summed).astype(BF16)


def on_device(
    activations, grad_out, kept_rows, kept_cols, kept_count, owner_tiles, apply_mask, feedback_in
):
    vmem = pl.BlockSpec(memory_space=pltpu.VMEM)
    smem = pl.BlockSpec(memory_space=pltpu.SMEM)
    table, code = pl.pallas_call(
        prep_kernel,
        out_shape=(
            jax.ShapeDtypeStruct((2, TILE), jnp.int32),
            jax.ShapeDtypeStruct((CORES, YN, TILE), F32),
        ),
        in_specs=[smem, vmem, vmem, vmem],
        out_specs=(vmem, vmem),
    )(kept_count, kept_rows, kept_cols, owner_tiles.reshape(-1, TILE))

    dma = pltpu.SemaphoreType.DMA
    summed = pl.pallas_call(
        main_kernel,
        out_shape=jax.ShapeDtypeStruct(feedback_in.shape, BF16),
        in_specs=[smem, vmem, vmem, vmem, vmem],
        out_specs=vmem,
        scratch_shapes=[
            pltpu.VMEM((activations.shape[1] // TILE, TILE, TILE), BF16),
            pltpu.VMEM((grad_out.shape[1] // TILE, TILE, TILE), BF16),
            pltpu.VMEM((PARTS, SLICES, 2 * SLOT, ROWS, TILE), BF16),
            pltpu.VMEM((PARTS, SLICES, CORES, 2 * SLOT, ROWS, TILE), BF16),
            pltpu.VMEM((PARTS, SLICES, CORES, 2 * SLOT, ROWS, TILE), BF16),
            pltpu.VMEM((CLUSTER, YN, TILE), F32),
            pltpu.VMEM((ZH, YN, CLUSTER * SLOT * ROWS), F32),
            pltpu.VMEM((ZH, PIECE, TILE), F32),
            pltpu.VMEM((ZH, 4, PIECE, TILE), BF16),
            pltpu.VMEM((ZH, 4, PIECE, TILE), BF16),
            pltpu.VMEM((ZH, 3, PIECE, TILE), BF16),
            pltpu.VMEM((ZH, 3, PIECE, TILE), BF16),
            pltpu.VMEM((ZH - 1, PIECE, TILE), BF16),
            pltpu.VMEM((ZH - 1, PIECE, TILE), BF16),
            dma((CLUSTER,)), dma((CLUSTER,)),
            dma((PARTS,)), dma((PARTS,)),
            dma((PARTS, SLICES)), dma((PARTS, SLICES)),
            dma((ZH, 4)), dma((ZH, 4)),
            dma((ZH, 3)), dma((ZH, 3)),
            dma((ZH - 1,)), dma((ZH - 1,)),
            dma((SLICES,)), dma((SLICES,)),
        ],
        compiler_params=pltpu.CompilerParams(
            collective_id=0, has_side_effects=True, vmem_limit_bytes=56 * 2**20
        ),
    )(table, code, activations, grad_out, feedback_in)
    some = pl.BlockSpec((5, TILE, TILE), lambda i: (i, 0, 0))
    return tuple(
        pl.pallas_call(
            split_kernel,
            grid=(feedback_in.shape[0] // 5,),
            out_shape=(jax.ShapeDtypeStruct(feedback_in.shape, BF16),) * 2,
            in_specs=[smem, some],
            out_specs=(some, some),
        )(apply_mask, summed)
    )


def solution(mesh):
    return jax.shard_map(
        on_device,
        mesh=mesh,
        in_specs=(
            P(("blk", "group"), None),
            P(("blk", "group"), None),
            P(("blk", "group"), None),
            P(("blk", "group"), None),
            P(("blk", "group")),
            P(),
            P("blk"),
            P("blk", None, None),
        ),
        out_specs=(P("blk", None, None), P("blk", None, None)),
        check_vma=False,
    )
```

time: 117 us -> 96.4 us (0.82)
  the two profiles are of different devices: /device:TPU:32 before, /device:TPU:1 now
where the time goes in v2:
time: 96.4 us; the launch traced here: 96.2 us
  Pallas kernels  94.9 us (98%)
  between operations  1.29 us (1%)
    pallas_call x1, Pallas kernels, on_device(): pl.pallas_call(main_kernel, out_shape=jax.ShapeDtypeStruct(feedback_in.sh...  89.6 us
    pallas_call x1, Pallas kernels, on_device(): pl.pallas_call(split_kernel, grid=(feedback_in.shape[0] // 5,), out_shape...  3.42 us

profile of v2, /device:TPU:1, one launch (start us, length us, event | category | flops | bytes accessed | tf_op | source)
XLA Modules:
  0.0 96.2 jit_solution(9500377991160497005)
XLA Ops:
  1.3 1.8 %shard_map.95 = (s32[2,128]{1,0:T(2,128)}, f32[2,8,128]{2,1,0:T(8,128)}) custom-call(s32[1]{0:T(128)S(6)} %copy.10.count_ref, s32[1,128]{1,0:T(1,128)} %rows_ref.1, s32[1,128]{1,0:T(1,128)} %cols_ref.1, s32[10,128]{1,0:T(8,128)} %bitcast.1), custom_call_target="tpu_custom_call" | custom-call | tf_op jit(solution)/shard_map/pallas_call | solution.py:297
  3.1 89.6 %shard_map.96.summed_ref = bf16[20,128,128]{2,1,0:T(8,128)(2,1)} custom-call(s32[2,128]{1,0:T(2,128)} %get-tuple-element.4.table_ref, f32[2,8,128]{2,1,0:T(8,128)} %get-tuple-element.5.code_ref, bf16[128,2560]{1,0:T(8,128)(2,1)} %act_ref.1, bf16[128,8192]{1,0:T(8,128)(2,1)} %grad_ref.1, bf16[20,128,128]{2,1,0:T(8,128)(2,1)} %back_ref.1), custom_call_target="tpu_custom_call" | custom-call | tf_op jit(solution)/shard_map/pallas_call | solution.py:308
  92.8 3.4 %shard_map.97 = (bf16[20,128,128]{2,1,0:T(8,128)(2,1)}, bf16[20,128,128]{2,1,0:T(8,128)(2,1)}) custom-call(s32[20]{0:T(128)} %mask_ref.1, bf16[20,128,128]{2,1,0:T(8,128)(2,1)} %shard_map.96.summed_ref), custom_call_target="tpu_custom_call" | custom-call | tf_op jit(solution)/shard_map/pallas_call | solution.py:342

commit v3 on v2

v3 whole, which is shorter than its diff:
```python
import functools

import jax
import jax.numpy as jnp
from jax import lax
from jax.experimental import pallas as pl
from jax.experimental.pallas import tpu as pltpu
from jax.sharding import PartitionSpec as P

ZH, YN, CORES, XN, ZL = 4, 8, 2, 4, 2
SLICES = XN * ZL
CLUSTER = SLICES * CORES
SLOT = 2
TILE = 128
ROWS = TILE // SLICES
OWNED = 20
PIECE = OWNED * ROWS
PER_CHUNK = YN * SLOT
PARTS = 16
AHEAD = 9
ORDER = (
    (0, 0), (0, 1), (1, 0), (0, 2), (1, 1), (0, 3), (1, 2), (2, 0),
    (1, 3), (2, 1), (3, 0), (2, 2), (3, 1), (2, 3), (3, 2), (3, 3),
)
SPLIT = 10
MESH = pl.DeviceIdType.MESH
F32 = jnp.float32
BF16 = jnp.bfloat16


def index_work(count_ref, rows_ref, cols_ref, tiles_ref, table_ref, code_ref):
    n = TILE
    sub = lax.broadcasted_iota(jnp.int32, (n, n), 0).astype(F32)
    lane = lax.broadcasted_iota(jnp.int32, (n, n), 1).astype(F32)
    count = count_ref[0].astype(F32)
    row_of = jnp.broadcast_to(rows_ref[...].astype(F32), (n, n)).T
    col_of = jnp.broadcast_to(cols_ref[...].astype(F32), (n, n)).T
    tile_of = row_of * 64.0 + col_of
    found = jnp.zeros((n, n), F32)
    for k in range(tiles_ref.shape[0]):
        known = tiles_ref[k : k + 1, :].astype(F32)
        found += jnp.where(tile_of == known, lane + 128.0 * k, 0.0)
    position = jnp.broadcast_to(jnp.sum(found, axis=1, keepdims=True), (n, n))
    owner = jnp.floor((position + 0.5) * (1.0 / OWNED))
    label = position - OWNED * owner
    same = (owner.T == owner) & (lane < sub) & (lane < count)
    rank = jnp.sum(jnp.where(same, 1.0, 0.0), axis=1, keepdims=True)
    z_hi = jnp.floor((owner + 0.5) * (1.0 / 16.0))
    in_plane = owner - 16.0 * z_hi
    y = jnp.floor((in_plane + 0.5) * 0.5)
    core = in_plane - 2.0 * y
    slot = ((z_hi * 2.0 + core) * 8.0 + y) * 2.0 + rank
    chosen = (slot == lane) & (sub < count)
    slot_row = jnp.sum(jnp.where(chosen, row_of, 0.0), axis=0, keepdims=True)
    slot_col = jnp.sum(jnp.where(chosen, col_of, 0.0), axis=0, keepdims=True)
    slot_label = jnp.sum(jnp.where(chosen, label + 1.0, 0.0), axis=0, keepdims=True) - 1.0
    table_ref[0:1, :] = slot_row.astype(jnp.int32)
    table_ref[1:2, :] = slot_col.astype(jnp.int32)
    m = CORES * YN
    at = lax.broadcasted_iota(jnp.int32, (m, n), 0)
    s = lax.broadcasted_iota(jnp.int32, (m, n), 1)
    mine = (s // 16) % 2 * 8 + (s // 2) % 8 == at
    spread = jnp.where(mine, jnp.broadcast_to(slot_label, (m, n)), 0.0).astype(BF16)
    s2 = lax.broadcasted_iota(jnp.int32, (n, n), 0)
    l2 = lax.broadcasted_iota(jnp.int32, (n, n), 1)
    pick = jnp.where((s2 // 32 == l2 // 32) & (s2 % 2 == l2 // 16 % 2), 1.0, 0.0).astype(BF16)
    coded = jnp.dot(spread, pick, preferred_element_type=F32) * 16.0
    coded += (lax.broadcasted_iota(jnp.int32, (m, n), 1) % 16).astype(F32)
    code_ref[...] = coded.reshape(CORES, YN, n)


def main_kernel(
    count_ref, rows_ref, cols_ref, tiles_ref, act_hbm, grad_hbm, back_hbm, out_ref,
    act_ref, grad_ref, back_ref, table_made, table_ref, code_ref,
    act_t, grad_t, other, made, got, codes, keys, own,
    to_right, from_left, to_left, from_right, to_z, from_z,
    load, code_send, code_recv, swap_send, swap_recv, made_send, made_recv,
    right_send, right_recv, left_send, left_recv, z_send, z_recv, out_send, out_recv,
):
    blk = lax.axis_index("blk")
    group = lax.axis_index("group")
    z_hi, y, core = blk // 16, (blk // 2) % 8, blk % 2
    x, z_lo = group // 2, group % 2
    me = group * 2 + core

    def device(z_hi_at, y_at, core_at, group_at):
        return ((z_hi_at * 8 + y_at) * 2 + core_at, group_at)

    def member(n, way):
        return ((x + way * (n // 2) + XN) % XN) * 2 + (z_lo + n % 2) % 2

    def remote(src, dst, send, recv, to):
        return pltpu.make_async_remote_copy(
            src_ref=src, dst_ref=dst, send_sem=send, recv_sem=recv,
            device_id=to, device_id_type=MESH,
        )

    def each(stop, do):
        def step(n, _):
            do(n)
            return 0

        lax.fori_loop(1, stop, step, 0)

    right = device(z_hi, (y + 1) % 8, core, group)
    left = device(z_hi, (y + 7) % 8, core, group)
    sibling = device(z_hi, y, 1 - core, group)

    loads = [
        pltpu.make_async_copy(there, here, load.at[i])
        for i, (there, here) in enumerate(
            [(act_hbm, act_ref), (grad_hbm, grad_ref), (back_hbm, back_ref)]
        )
    ]
    for copy in loads:
        copy.start()

    barrier = pltpu.get_barrier_semaphore()

    def greet(to):
        pl.semaphore_signal(barrier, inc=1, device_id=to, device_id_type=MESH)

    greet(sibling)
    each(SLICES, lambda n: greet(device(z_hi, y, core, member(n, 1))))
    greet(right)
    greet(left)
    each(ZH, lambda k: greet(device((z_hi + k) % 4, y, core, group)))

    index_work(count_ref, rows_ref, cols_ref, tiles_ref, table_made, code_ref)
    table = pltpu.make_async_copy(table_made, table_ref, load.at[3])
    table.start()
    loads[0].wait()

    def turn(r, _):
        act_t[r] = act_ref[:, pl.ds(pl.multiple_of(r * TILE, TILE), TILE)].T
        return 0

    lax.fori_loop(0, act_ref.shape[1] // TILE, turn, 0, unroll=4)

    loads[1].wait()

    def part(r, _):
        grad_t[r] = grad_ref[:, pl.ds(pl.multiple_of(r * TILE, TILE), TILE)]
        return 0

    lax.fori_loop(0, grad_ref.shape[1] // TILE, part, 0, unroll=4)

    def plane(k):
        return (z_hi + 1 + k) % 4

    def pair(p):
        return (y + 4 - p) % 8, (y + 5 + p) % 8

    def make(m):
        k, p = ORDER[m]

        def tile(core_to, o, j):
            e = (plane(k) * 2 + core_to) * PER_CHUNK + pair(p)[o] * SLOT + j
            r = jnp.clip(table_ref[0, e], 0, act_t.shape[0] - 1)
            c = jnp.clip(table_ref[1, e], 0, grad_t.shape[0] - 1)
            a, b = act_t[r], grad_t[c]
            product = jnp.dot(a, b, preferred_element_type=F32).astype(BF16)
            return product.reshape(SLICES, ROWS, TILE)

        for o in range(2):
            for j in range(SLOT):
                other[m, :, o * SLOT + j] = tile(1 - core, o, j)
        for o in range(2):
            for j in range(SLOT):
                made[m, :, core, o * SLOT + j] = tile(core, o, j)

    def code_swap(way):
        there = codes.at[group, core if way == 1 else 1 - core]
        return remote(code_ref.at[1 - core], there, code_send.at[0], code_recv.at[0], sibling)

    def code_copy(n):
        mine = codes.at[group]
        to = device(z_hi, y, core, member(n, 1))
        return remote(mine, mine, code_send.at[1], code_recv.at[1], to)

    def swap(m, way):
        there = made.at[m, :, core if way == 1 else 1 - core]
        return remote(other.at[m], there, swap_send.at[0], swap_recv.at[m], sibling)

    def made_copy(m, n):
        to = device(z_hi, y, core, member(n, 1))
        return remote(made.at[m, member(n, 1)], got.at[m, group], made_send.at[0], made_recv.at[m], to)

    def all_of(ref, semaphore):
        pltpu.make_async_copy(ref, ref, semaphore).wait()

    def right_copy(k, s):
        return remote(
            to_right.at[k, s], from_left.at[k, s], right_send.at[0], right_recv.at[k, s], right
        )

    def left_copy(k, s):
        return remote(
            to_left.at[k, s], from_right.at[k, s], left_send.at[0], left_recv.at[k, s], left
        )

    def z_copy(k):
        to = device(plane(k), y, core, group)
        return remote(to_z.at[k], from_z.at[k], z_send.at[0], z_recv.at[k], to)

    def out_copy(n):
        there = out_ref.at[group]
        to = device(z_hi, y, core, member(n, 1))
        return remote(there, there, out_send.at[0], out_recv.at[0], to)

    def send(m):
        swap(m, -1).wait_recv()
        each(SLICES, lambda n: made_copy(m, n).start())

    lane = lax.broadcasted_iota(jnp.int32, (YN, TILE), 1)
    row = lax.broadcasted_iota(jnp.int32, (PIECE, CLUSTER * SLOT * ROWS), 0).astype(F32)

    def line_up(k):
        for kk in range(4):
            key = jnp.zeros((YN, TILE), F32)
            for i in range(4):
                turned = pltpu.roll(codes[kk * 2 + i // 2, i % 2], (i + 4 - plane(k)) % 4 * 32, 1)
                key = jnp.where(lane // 32 == i, turned, key)
            keys[k, :, kk * TILE : (kk + 1) * TILE] = key

    def owner_sum(m, o):
        k, p = ORDER[m]
        pick = jnp.where(row == keys[k, pl.ds(pair(p)[o], 1), :], 1.0, 0.0).astype(BF16)
        parts = got[m, :, :, o * SLOT : (o + 1) * SLOT].reshape(CLUSTER * SLOT * ROWS, TILE)
        return jnp.dot(pick, parts, preferred_element_type=F32)

    def finish(k):
        left_copy(k, 2).wait_recv()
        right_copy(k, 3).wait_recv()
        total = own[k] + from_right[k, 2].astype(F32) + from_left[k, 3].astype(F32)
        if k < ZH - 1:
            to_z[k] = total.astype(BF16)
            z_copy(k).start()
        return total

    table.wait()
    make(0)
    pl.semaphore_wait(barrier, 1 + SLICES - 1 + 2 + ZH - 1)
    swap(0, 1).start()
    code_swap(1).start()
    codes[group, core] = code_ref[core]
    for m in range(1, AHEAD + 1):
        make(m)
        swap(m, 1).start()
        send(m - 1)
        if m == 1:
            code_swap(-1).wait_recv()
            each(SLICES, lambda n: code_copy(n).start())
    all_of(codes.at[1:], code_recv.at[1])
    for k in range(ZH):
        line_up(k)

    total = None
    for m in range(PARTS):
        k, p = ORDER[m]
        if m + AHEAD + 1 < PARTS:
            make(m + AHEAD + 1)
            swap(m + AHEAD + 1, 1).start()
        if m + AHEAD < PARTS:
            send(m + AHEAD)
        got[m, group] = made[m, group]
        all_of(got.at[m, 1:], made_recv.at[m])
        rightward = owner_sum(m, 0)
        if p > 0:
            right_copy(k, p - 1).wait_recv()
            rightward += from_left[k, p - 1].astype(F32)
        to_right[k, p] = rightward.astype(BF16)
        right_copy(k, p).start()
        leftward = owner_sum(m, 1)
        if p < 3:
            if p > 0:
                left_copy(k, p - 1).wait_recv()
                leftward += from_right[k, p - 1].astype(F32)
            to_left[k, p] = leftward.astype(BF16)
            left_copy(k, p).start()
        else:
            own[k] = leftward
        if m > 0 and ORDER[m - 1][1] == 3:
            finish(ORDER[m - 1][0])
    total = finish(ZH - 1)

    for k in range(ZH - 1):
        z_copy(k).wait_recv()
        total += from_z[k].astype(F32)
    loads[2].wait()
    mine = pl.ds(pl.multiple_of(group * ROWS, ROWS), ROWS)
    total += back_ref[:, mine, :].astype(F32).reshape(PIECE, TILE)
    out_ref[group] = total.astype(BF16).reshape(OWNED, ROWS, TILE)
    each(SLICES, lambda n: out_copy(n).start())
    all_of(out_ref.at[1:], out_recv.at[0])

    code_swap(1).wait_send()
    all_of(codes.at[1:], code_send.at[1])
    all_of(other, swap_send.at[0])
    all_of(made.at[: PARTS * (SLICES - 1) // SLICES], made_send.at[0])
    all_of(to_right, right_send.at[0])
    all_of(to_left, left_send.at[0])
    all_of(to_z, z_send.at[0])
    all_of(out_ref.at[1:], out_send.at[0])


def split_kernel(mask_ref, summed_ref, update_ref, feedback_ref):
    tiles = update_ref.shape[0]
    for t in range(tiles):
        applied = mask_ref[pl.program_id(0) * tiles + t] == 1
        for g in range(SLICES):
            summed = summed_ref[g, t].astype(F32)
            at = slice(g * ROWS, (g + 1) * ROWS)
            update_ref[t, at] = jnp.where(applied, summed, 0.0).astype(BF16)
            feedback_ref[t, at] = jnp.where(applied, 0.0, summed).astype(BF16)


def on_device(
    activations, grad_out, kept_rows, kept_cols, kept_count, owner_tiles, apply_mask, feedback_in
):
    vmem = pl.BlockSpec(memory_space=pltpu.VMEM)
    smem = pl.BlockSpec(memory_space=pltpu.SMEM)
    anywhere = pl.BlockSpec(memory_space=pl.ANY)
    dma = pltpu.SemaphoreType.DMA
    summed = pl.pallas_call(
        main_kernel,
        out_shape=jax.ShapeDtypeStruct((SLICES, OWNED, ROWS, TILE), BF16),
        in_specs=[smem, vmem, vmem, vmem, anywhere, anywhere, anywhere],
        out_specs=vmem,
        scratch_shapes=[
            pltpu.VMEM(activations.shape, BF16),
            pltpu.VMEM(grad_out.shape, BF16),
            pltpu.VMEM(feedback_in.shape, BF16),
            pltpu.VMEM((2, TILE), jnp.int32),
            pltpu.SMEM((2, TILE), jnp.int32),
            pltpu.VMEM((CORES, YN, TILE), F32),
            pltpu.VMEM((activations.shape[1] // TILE, TILE, TILE), BF16),
            pltpu.VMEM((grad_out.shape[1] // TILE, TILE, TILE), BF16),
            pltpu.VMEM((PARTS, SLICES, 2 * SLOT, ROWS, TILE), BF16),
            pltpu.VMEM((PARTS, SLICES, CORES, 2 * SLOT, ROWS, TILE), BF16),
            pltpu.VMEM((PARTS, SLICES, CORES, 2 * SLOT, ROWS, TILE), BF16),
            pltpu.VMEM((SLICES, CORES, YN, TILE), F32),
            pltpu.VMEM((ZH, YN, CLUSTER * SLOT * ROWS), F32),
            pltpu.VMEM((ZH, PIECE, TILE), F32),
            pltpu.VMEM((ZH, 4, PIECE, TILE), BF16),
            pltpu.VMEM((ZH, 4, PIECE, TILE), BF16),
            pltpu.VMEM((ZH, 3, PIECE, TILE), BF16),
            pltpu.VMEM((ZH, 3, PIECE, TILE), BF16),
            pltpu.VMEM((ZH - 1, PIECE, TILE), BF16),
            pltpu.VMEM((ZH - 1, PIECE, TILE), BF16),
            dma((4,)),
            dma((2,)), dma((2,)),
            dma((1,)), dma((PARTS,)),
            dma((1,)), dma((PARTS,)),
            dma((1,)), dma((ZH, 4)),
            dma((1,)), dma((ZH, 3)),
            dma((1,)), dma((ZH - 1,)),
            dma((1,)), dma((1,)),
        ],
        compiler_params=pltpu.CompilerParams(
            collective_id=0, has_side_effects=True, vmem_limit_bytes=56 * 2**20
        ),
    )(
        kept_count, kept_rows, kept_cols, owner_tiles.reshape(-1, TILE),
        activations, grad_out, feedback_in,
    )
    some = pl.BlockSpec((SPLIT, TILE, TILE), lambda i: (i, 0, 0))
    return tuple(
        pl.pallas_call(
            split_kernel,
            grid=(OWNED // SPLIT,),
            out_shape=(jax.ShapeDtypeStruct(feedback_in.shape, BF16),) * 2,
            in_specs=[smem, pl.BlockSpec((SLICES, SPLIT, ROWS, TILE), lambda i: (0, i, 0, 0))],
            out_specs=(some, some),
        )(apply_mask, summed)
    )


def solution(mesh):
    return jax.shard_map(
        on_device,
        mesh=mesh,
        in_specs=(
            P(("blk", "group"), None),
            P(("blk", "group"), None),
            P(("blk", "group"), None),
            P(("blk", "group"), None),
            P(("blk", "group")),
            P(),
            P("blk"),
            P("blk", None, None),
        ),
        out_specs=(P("blk", None, None), P("blk", None, None)),
        check_vma=False,
    )
```

time: 96.4 us -> 84.5 us (0.88)
  Pallas kernels: 94.9 us -> 82.3 us
    pallas_call x3 -> x2, Pallas kernels: 94.9 us -> 82.3 us  [the longest x1 80.2 us: on_device(): pl.pallas_call(main_kernel, out_shape=jax.ShapeDtypeStruct((SLICES, OWNED...]
where the time goes in v3:
time: 84.5 us; the launch traced here: 83.6 us
  Pallas kernels  82.3 us (97%)
  between operations  1.29 us (2%)
    pallas_call x1, Pallas kernels, on_device(): pl.pallas_call(main_kernel, out_shape=jax.ShapeDtypeStruct((SLICES, OWNED...  80.2 us
    pallas_call x1, Pallas kernels, on_device(): pl.pallas_call(split_kernel, grid=(OWNED // SPLIT,), out_shape=(jax.Shape...  2.14 us

profile of v3, /device:TPU:1, one launch (start us, length us, event | category | flops | bytes accessed | tf_op | source)
XLA Modules:
  0.0 83.6 jit_solution(13566792757437348794)
XLA Ops:
  1.3 80.2 %shard_map.95.summed_ref = bf16[8,20,16,128]{3,2,1,0:T(8,128)(2,1)} custom-call(s32[1]{0:T(128)S(6)} %copy.10.count_ref, s32[1,128]{1,0:T(1,128)} %rows_ref.1, s32[1,128]{1,0:T(1,128)} %cols_ref.1, s32[10,128]{1,0:T(8,128)} %bitcast.1, bf16[128,2560]{1,0:T(8,128)(2,1)} %act_hbm.1, bf16[128,8192]{1,0:T(8,128)(2,1)} %grad_hbm.1, bf16[20,128,128]{2,1,0:T(8,128)(2,1)} %back_hbm.1), custom_call_target="tpu_custom_call" | custom-call | tf_op jit(solution)/shard_map/pallas_call | solution.py:325
  81.5 2.1 %shard_map.96 = (bf16[20,128,128]{2,1,0:T(8,128)(2,1)}, bf16[20,128,128]{2,1,0:T(8,128)(2,1)}) custom-call(s32[20]{0:T(128)} %mask_ref.1, bf16[8,20,16,128]{3,2,1,0:T(8,128)(2,1)} %shard_map.95.summed_ref), custom_call_target="tpu_custom_call" | custom-call | tf_op jit(solution)/shard_map/pallas_call | solution.py:369

commit v4 on v3

--- a/solution.py
+++ b/solution.py
@@ -19,10 +19,11 @@
 PARTS = 16
 AHEAD = 9
 ORDER = (
-    (0, 0), (0, 1), (1, 0), (0, 2), (1, 1), (0, 3), (1, 2), (2, 0),
-    (1, 3), (2, 1), (3, 0), (2, 2), (3, 1), (2, 3), (3, 2), (3, 3),
+    (0, 0), (1, 0), (2, 0), (0, 1), (1, 1), (2, 1), (0, 2), (1, 2),
+    (3, 0), (2, 2), (0, 3), (3, 1), (2, 3), (1, 3), (3, 2), (3, 3),
 )
-SPLIT = 10
+FAR_FIRST = (4, 5, 2, 6, 3, 7, 1)
+HALF = PIECE // 2
 MESH = pl.DeviceIdType.MESH
 F32 = jnp.float32
 BF16 = jnp.bfloat16
@@ -75,7 +76,7 @@
     act_t, grad_t, other, made, got, codes, keys, own,
     to_right, from_left, to_left, from_right, to_z, from_z,
     load, code_send, code_recv, swap_send, swap_recv, made_send, made_recv,
-    right_send, right_recv, left_send, left_recv, z_send, z_recv, out_send, out_recv,
+    right_send, right_recv, last_recv, left_send, left_recv, z_send, z_recv, out_send, out_recv,
 ):
     blk = lax.axis_index("blk")
     group = lax.axis_index("group")
@@ -182,9 +183,11 @@
         there = made.at[m, :, core if way == 1 else 1 - core]
         return remote(other.at[m], there, swap_send.at[0], swap_recv.at[m], sibling)
 
-    def made_copy(m, n):
-        to = device(z_hi, y, core, member(n, 1))
-        return remote(made.at[m, member(n, 1)], got.at[m, group], made_send.at[0], made_recv.at[m], to)
+    def made_copy(m, n, part, semaphore):
+        g = member(n, 1)
+        src, dst = made.at[(m, g, *part)], got.at[(m, group, *part)]
+        to = device(z_hi, y, core, g)
+        return remote(src, dst, made_send.at[0], made_recv.at[semaphore], to)
 
     def all_of(ref, semaphore):
         pltpu.make_async_copy(ref, ref, semaphore).wait()
@@ -203,14 +206,27 @@
         to = device(plane(k), y, core, group)
         return remote(to_z.at[k], from_z.at[k], z_send.at[0], z_recv.at[k], to)
 
-    def out_copy(n):
-        there = out_ref.at[group]
+    def out_copy(h, n):
+        there = out_ref.at[h, group]
         to = device(z_hi, y, core, member(n, 1))
-        return remote(there, there, out_send.at[0], out_recv.at[0], to)
+        return remote(there, there, out_send.at[0], out_recv.at[h], to)
+
+    def last_copy(h):
+        at = (ZH - 1, 3, slice(h * HALF, (h + 1) * HALF))
+        return remote(
+            to_right.at[at], from_left.at[at], right_send.at[0], last_recv.at[h], right
+        )
 
     def send(m):
         swap(m, -1).wait_recv()
-        each(SLICES, lambda n: made_copy(m, n).start())
+        if m == 0:
+            each(SLICES, lambda n: made_copy(m, n, (1 - core,), m).start())
+        elif m < PARTS - 1:
+            each(SLICES, lambda n: made_copy(m, n, (), m).start())
+        else:
+            for o in range(2):
+                part = (slice(None), slice(o * SLOT, (o + 1) * SLOT))
+                each(SLICES, lambda n, o=o, part=part: made_copy(m, n, part, m + o).start())
 
     lane = lax.broadcasted_iota(jnp.int32, (YN, TILE), 1)
     row = lax.broadcasted_iota(jnp.int32, (PIECE, CLUSTER * SLOT * ROWS), 0).astype(F32)
@@ -223,9 +239,9 @@
                 key = jnp.where(lane // 32 == i, turned, key)
             keys[k, :, kk * TILE : (kk + 1) * TILE] = key
 
-    def owner_sum(m, o):
+    def owner_sum(m, o, rows=slice(None)):
         k, p = ORDER[m]
-        pick = jnp.where(row == keys[k, pl.ds(pair(p)[o], 1), :], 1.0, 0.0).astype(BF16)
+        pick = jnp.where(row[rows] == keys[k, pl.ds(pair(p)[o], 1), :], 1.0, 0.0).astype(BF16)
         parts = got[m, :, :, o * SLOT : (o + 1) * SLOT].reshape(CLUSTER * SLOT * ROWS, TILE)
         return jnp.dot(pick, parts, preferred_element_type=F32)
 
@@ -233,15 +249,14 @@
         left_copy(k, 2).wait_recv()
         right_copy(k, 3).wait_recv()
         total = own[k] + from_right[k, 2].astype(F32) + from_left[k, 3].astype(F32)
-        if k < ZH - 1:
-            to_z[k] = total.astype(BF16)
-            z_copy(k).start()
-        return total
+        to_z[k] = total.astype(BF16)
+        z_copy(k).start()
 
     table.wait()
     make(0)
     pl.semaphore_wait(barrier, 1 + SLICES - 1 + 2 + ZH - 1)
     swap(0, 1).start()
+    each(SLICES, lambda n: made_copy(0, n, (core,), 0).start())
     code_swap(1).start()
     codes[group, core] = code_ref[core]
     for m in range(1, AHEAD + 1):
@@ -255,8 +270,7 @@
     for k in range(ZH):
         line_up(k)
 
-    total = None
-    for m in range(PARTS):
+    for m in range(PARTS - 1):
         k, p = ORDER[m]
         if m + AHEAD + 1 < PARTS:
             make(m + AHEAD + 1)
@@ -282,17 +296,35 @@
             own[k] = leftward
         if m > 0 and ORDER[m - 1][1] == 3:
             finish(ORDER[m - 1][0])
-    total = finish(ZH - 1)
-
-    for k in range(ZH - 1):
-        z_copy(k).wait_recv()
-        total += from_z[k].astype(F32)
+    m, k = PARTS - 1, ZH - 1
+    got[m, group] = made[m, group]
+    all_of(got.at[m, 1:, :, :SLOT], made_recv.at[m])
+    right_copy(k, 2).wait_recv()
+    for h in range(2):
+        rows = slice(h * HALF, (h + 1) * HALF)
+        rightward = owner_sum(m, 0, rows) + from_left[k, 2, rows].astype(F32)
+        to_right[k, 3, rows] = rightward.astype(BF16)
+        last_copy(h).start()
+    all_of(got.at[m, 1:, :, SLOT:], made_recv.at[m + 1])
+    total = owner_sum(m, 1)
+    left_copy(k, 2).wait_recv()
+    total += from_right[k, 2].astype(F32)
     loads[2].wait()
     mine = pl.ds(pl.multiple_of(group * ROWS, ROWS), ROWS)
     total += back_ref[:, mine, :].astype(F32).reshape(PIECE, TILE)
-    out_ref[group] = total.astype(BF16).reshape(OWNED, ROWS, TILE)
-    each(SLICES, lambda n: out_copy(n).start())
-    all_of(out_ref.at[1:], out_recv.at[0])
+    for z in range(ZH - 1):
+        z_copy(z).wait_recv()
+        total += from_z[z].astype(F32)
+    own[k] = total
+    for h in range(2):
+        rows = slice(h * HALF, (h + 1) * HALF)
+        last_copy(h).wait_recv()
+        total = own[k, rows] + from_left[k, 3, rows].astype(F32)
+        out_ref[h, group] = total.astype(BF16).reshape(OWNED // 2, ROWS, TILE)
+        for n in FAR_FIRST:
+            out_copy(h, n).start()
+    for h in range(2):
+        all_of(out_ref.at[h, 1:], out_recv.at[h])
 
     code_swap(1).wait_send()
     all_of(codes.at[1:], code_send.at[1])
@@ -301,7 +333,7 @@
     all_of(to_right, right_send.at[0])
     all_of(to_left, left_send.at[0])
     all_of(to_z, z_send.at[0])
-    all_of(out_ref.at[1:], out_send.at[0])
+    all_of(out_ref.at[:, 1:], out_send.at[0])
 
 
 def split_kernel(mask_ref, summed_ref, update_ref, feedback_ref):
@@ -309,7 +341,7 @@
     for t in range(tiles):
         applied = mask_ref[pl.program_id(0) * tiles + t] == 1
         for g in range(SLICES):
-            summed = summed_ref[g, t].astype(F32)
+            summed = summed_ref[0, g, t].astype(F32)
             at = slice(g * ROWS, (g + 1) * ROWS)
             update_ref[t, at] = jnp.where(applied, summed, 0.0).astype(BF16)
             feedback_ref[t, at] = jnp.where(applied, 0.0, summed).astype(BF16)
@@ -324,7 +356,7 @@
     dma = pltpu.SemaphoreType.DMA
     summed = pl.pallas_call(
         main_kernel,
-        out_shape=jax.ShapeDtypeStruct((SLICES, OWNED, ROWS, TILE), BF16),
+        out_shape=jax.ShapeDtypeStruct((2, SLICES, OWNED // 2, ROWS, TILE), BF16),
         in_specs=[smem, vmem, vmem, vmem, anywhere, anywhere, anywhere],
         out_specs=vmem,
         scratch_shapes=[
@@ -351,11 +383,11 @@
             dma((4,)),
             dma((2,)), dma((2,)),
             dma((1,)), dma((PARTS,)),
-            dma((1,)), dma((PARTS,)),
-            dma((1,)), dma((ZH, 4)),
+            dma((1,)), dma((PARTS + 1,)),
+            dma((1,)), dma((ZH, 4)), dma((2,)),
             dma((1,)), dma((ZH, 3)),
             dma((1,)), dma((ZH - 1,)),
-            dma((1,)), dma((1,)),
+            dma((1,)), dma((2,)),
         ],
         compiler_params=pltpu.CompilerParams(
             collective_id=0, has_side_effects=True, vmem_limit_bytes=56 * 2**20
@@ -364,14 +396,15 @@
         kept_count, kept_rows, kept_cols, owner_tiles.reshape(-1, TILE),
         activations, grad_out, feedback_in,
     )
-    some = pl.BlockSpec((SPLIT, TILE, TILE), lambda i: (i, 0, 0))
+    half = pl.BlockSpec((OWNED // 2, TILE, TILE), lambda i: (i, 0, 0))
+    pieces = pl.BlockSpec((1, SLICES, OWNED // 2, ROWS, TILE), lambda i: (i, 0, 0, 0, 0))
     return tuple(
         pl.pallas_call(
             split_kernel,
-            grid=(OWNED // SPLIT,),
+            grid=(2,),
             out_shape=(jax.ShapeDtypeStruct(feedback_in.shape, BF16),) * 2,
-            in_specs=[smem, pl.BlockSpec((SLICES, SPLIT, ROWS, TILE), lambda i: (0, i, 0, 0))],
-            out_specs=(some, some),
+            in_specs=[smem, pieces],
+            out_specs=(half, half),
         )(apply_mask, summed)
     )
 

time: 84.5 us -> 82 us (0.970)
  Pallas kernels: 82.3 us -> 79.2 us
    pallas_call x2, Pallas kernels: 82.3 us -> 79.2 us  [the longest x1 77.1 us: on_device(): pl.pallas_call(main_kernel, out_shape=jax.ShapeDtypeStruct((2, SLICES, OW...]
where the time goes in v4:
time: 82 us; the launch traced here: 80.5 us
  Pallas kernels  79.2 us (97%)
  between operations  1.29 us (2%)
    pallas_call x1, Pallas kernels, on_device(): pl.pallas_call(main_kernel, out_shape=jax.ShapeDtypeStruct((2, SLICES, OW...  77.1 us
    pallas_call x1, Pallas kernels, on_device(): pl.pallas_call(split_kernel, grid=(2,), out_shape=(jax.ShapeDtypeStruct(f...  2.14 us

profile of v4, /device:TPU:1, one launch (start us, length us, event | category | flops | bytes accessed | tf_op | source)
XLA Modules:
  0.0 80.5 jit_solution(3084556777635103683)
XLA Ops:
  1.3 77.1 %shard_map.95.summed_ref = bf16[2,8,10,16,128]{4,3,2,1,0:T(8,128)(2,1)} custom-call(s32[1]{0:T(128)S(6)} %copy.10.count_ref, s32[1,128]{1,0:T(1,128)} %rows_ref.1, s32[1,128]{1,0:T(1,128)} %cols_ref.1, s32[10,128]{1,0:T(8,128)} %bitcast.1, bf16[128,2560]{1,0:T(8,128)(2,1)} %act_hbm.1, bf16[128,8192]{1,0:T(8,128)(2,1)} %grad_hbm.1, bf16[20,128,128]{2,1,0:T(8,128)(2,1)} %back_hbm.1), custom_call_target="tpu_custom_call" | custom-call | tf_op jit(solution)/shard_map/pallas_call | solution.py:357
  78.4 2.1 %shard_map.96 = (bf16[20,128,128]{2,1,0:T(8,128)(2,1)}, bf16[20,128,128]{2,1,0:T(8,128)(2,1)}) custom-call(s32[20]{0:T(128)} %mask_ref.1, bf16[2,8,10,16,128]{4,3,2,1,0:T(8,128)(2,1)} %shard_map.95.summed_ref), custom_call_target="tpu_custom_call" | custom-call | tf_op jit(solution)/shard_map/pallas_call | solution.py:402

commit v5 on v4

--- a/solution.py
+++ b/solution.py
@@ -17,7 +17,7 @@
 PIECE = OWNED * ROWS
 PER_CHUNK = YN * SLOT
 PARTS = 16
-AHEAD = 9
+AHEAD = 11
 ORDER = (
     (0, 0), (1, 0), (2, 0), (0, 1), (1, 1), (2, 1), (0, 2), (1, 2),
     (3, 0), (2, 2), (0, 3), (3, 1), (2, 3), (1, 3), (3, 2), (3, 3),
@@ -219,10 +219,8 @@
 
     def send(m):
         swap(m, -1).wait_recv()
-        if m == 0:
+        if m < PARTS - 1:
             each(SLICES, lambda n: made_copy(m, n, (1 - core,), m).start())
-        elif m < PARTS - 1:
-            each(SLICES, lambda n: made_copy(m, n, (), m).start())
         else:
             for o in range(2):
                 part = (slice(None), slice(o * SLOT, (o + 1) * SLOT))
@@ -239,6 +237,10 @@
                 key = jnp.where(lane // 32 == i, turned, key)
             keys[k, :, kk * TILE : (kk + 1) * TILE] = key
 
+    def send_own(m):
+        if m < PARTS - 1:
+            each(SLICES, lambda n: made_copy(m, n, (core,), m).start())
+
     def owner_sum(m, o, rows=slice(None)):
         k, p = ORDER[m]
         pick = jnp.where(row[rows] == keys[k, pl.ds(pair(p)[o], 1), :], 1.0, 0.0).astype(BF16)
@@ -256,12 +258,13 @@
     make(0)
     pl.semaphore_wait(barrier, 1 + SLICES - 1 + 2 + ZH - 1)
     swap(0, 1).start()
-    each(SLICES, lambda n: made_copy(0, n, (core,), 0).start())
+    send_own(0)
     code_swap(1).start()
     codes[group, core] = code_ref[core]
     for m in range(1, AHEAD + 1):
         make(m)
         swap(m, 1).start()
+        send_own(m)
         send(m - 1)
         if m == 1:
             code_swap(-1).wait_recv()
@@ -275,6 +278,7 @@
         if m + AHEAD + 1 < PARTS:
             make(m + AHEAD + 1)
             swap(m + AHEAD + 1, 1).start()
+            send_own(m + AHEAD + 1)
         if m + AHEAD < PARTS:
             send(m + AHEAD)
         got[m, group] = made[m, group]

time: 82 us -> 82 us (level); the launches traced: 80.5 us -> 81.4 us
  Pallas kernels: 79.2 us -> 80.1 us
    pallas_call x1, Pallas kernels: 77.1 us -> 77.9 us  [on_device(): pl.pallas_call(main_kernel, out_shape=jax.ShapeDtypeStruct((2, SLICES, OW...]
where the time goes in v5:
time: 82 us; the launch traced here: 81.4 us
  Pallas kernels  80.1 us (98%)
  between operations  1.29 us (2%)
    pallas_call x1, Pallas kernels, on_device(): pl.pallas_call(main_kernel, out_shape=jax.ShapeDtypeStruct((2, SLICES, OW...  77.9 us
    pallas_call x1, Pallas kernels, on_device(): pl.pallas_call(split_kernel, grid=(2,), out_shape=(jax.ShapeDtypeStruct(f...  2.14 us

profile of v5, /device:TPU:1, one launch (start us, length us, event | category | flops | bytes accessed | tf_op | source)
XLA Modules:
  0.0 81.4 jit_solution(7299159284355286058)
XLA Ops:
  1.3 77.9 %shard_map.95.summed_ref = bf16[2,8,10,16,128]{4,3,2,1,0:T(8,128)(2,1)} custom-call(s32[1]{0:T(128)S(6)} %copy.10.count_ref, s32[1,128]{1,0:T(1,128)} %rows_ref.1, s32[1,128]{1,0:T(1,128)} %cols_ref.1, s32[10,128]{1,0:T(8,128)} %bitcast.1, bf16[128,2560]{1,0:T(8,128)(2,1)} %act_hbm.1, bf16[128,8192]{1,0:T(8,128)(2,1)} %grad_hbm.1, bf16[20,128,128]{2,1,0:T(8,128)(2,1)} %back_hbm.1), custom_call_target="tpu_custom_call" | custom-call | tf_op jit(solution)/shard_map/pallas_call | solution.py:361
  79.2 2.1 %shard_map.96 = (bf16[20,128,128]{2,1,0:T(8,128)(2,1)}, bf16[20,128,128]{2,1,0:T(8,128)(2,1)}) custom-call(s32[20]{0:T(128)} %mask_ref.1, bf16[2,8,10,16,128]{4,3,2,1,0:T(8,128)(2,1)} %shard_map.95.summed_ref), custom_call_target="tpu_custom_call" | custom-call | tf_op jit(solution)/shard_map/pallas_call | solution.py:406
